TPU v7x, 32 devices: a whole 2x2x4 slice. The times are simulated.
32 devices in a mesh: group: 2 (over y), att: 4 (over z), ffn: 4 (over x, core).
Axes of the slice: x: 2, y: 2, z: 4, core: 2. Of those that a mesh axis runs over, the one named last changes fastest.
Arguments:
- hidden_state: bfloat16 [160, 8192], P(('group', 'att'), 'ffn'), parts along dimension 0, may hold values from -40 to 40
- queries: bfloat16 [160, 8192], P(('group', 'att'), 'ffn'), parts along dimension 0, may hold values from -800 to 800
- key_cache: bfloat16 [102400, 1024], P(('group', 'att'), 'ffn'), parts along dimension 0, may hold values from -6 to 6
- value_cache: bfloat16 [102400, 1024], P(('group', 'att'), 'ffn'), parts along dimension 0, may hold values from -6 to 6
- lengths: int32 [160], P(('group', 'att')), parts along dimension 0, may hold values from 1 to 1279, as said below
- assignment: int32 [160], P('group'), parts along dimension 0, may hold values from 0 to 79, each once
- out_weight: bfloat16 [8, 1024, 8192], P(None, 'att', 'ffn'), may hold values from -0.375 to 0.375
- norm_gain: bfloat16 [8192], P('ffn'), may hold values from 0.099609375 to 1.8984375
- gate_weight: bfloat16 [14336, 8192], P('att', 'ffn'), may hold values from -0.0625 to 0.0625
- up_weight: bfloat16 [14336, 8192], P('att', 'ffn'), may hold values from -0.0625 to 0.0625
- down_weight: bfloat16 [14336, 8192], P('att', 'ffn'), may hold values from -0.0625 to 0.0625
Outputs:
- next_hidden: bfloat16 [160, 8192], P(('group', 'att'), 'ffn'), parts along dimension 0
There are 2 independent parts, one for each index of `group`. A program takes and returns all parts, laid end to end along the dimension named above; an argument that names none is the same for every part. Nothing has to cross between parts.
Inputs may be any that keep to these rules, and one draw needn't show every extreme that they name: Each attention index holds the contexts of its 20 slots end to end in its 12800 cache rows in slot order; their lengths sum to at most 12800, and to exactly 12800 on some attention index in every draw. `assignment`: A permutation of the requests.
All inputs are finite; a program needn't handle non-finite values.
Results may differ from a plain program's by a relative error of at most 0.02.
Values may be sent and summed in bfloat16 or wider, within the bound.
A program may use at most 192 MiB of HBM per device.

v0:
```python
import math

import jax
import jax.numpy as jnp
from jax import lax
from jax.sharding import PartitionSpec as P

epsilon = 1e-05
masked_score = -1e30


def softmax_rounded(scores):
    row_top = jnp.max(scores, axis=-1, keepdims=True)
    shifted = jnp.exp(scores - row_top)
    totals = jnp.sum(shifted, axis=-1, keepdims=True)
    return (shifted / totals).astype(jnp.bfloat16)


def per_device(
    hidden_state,
    queries,
    key_cache,
    value_cache,
    lengths,
    assignment,
    out_weight,
    norm_gain,
    gate_weight,
    up_weight,
    down_weight,
):
    rows_dev = hidden_state.shape[0]
    columns = hidden_state.shape[1]
    att_count = lax.axis_size("att")
    ffn_count = lax.axis_size("ffn")
    requests = rows_dev * att_count
    kv_total = out_weight.shape[0]
    kv_local = kv_total // ffn_count
    model_width = columns * ffn_count
    pool_rows = key_cache.shape[0]
    head_size = key_cache.shape[1] // kv_local
    per_group = queries.shape[1] // (kv_local * head_size)
    score_scale = 1.0 / math.sqrt(head_size)
    att_place = lax.axis_index("att")
    every_query = lax.all_gather(queries, "att", axis=0, tiled=True)
    own_slots = lax.dynamic_slice_in_dim(assignment, att_place * rows_dev, rows_dev)
    slot_queries = jnp.take(every_query, own_slots, axis=0).reshape(
        rows_dev, kv_local, per_group, head_size
    )
    keys_local = key_cache.reshape(pool_rows, kv_local, head_size)
    values_local = value_cache.reshape(pool_rows, kv_local, head_size)
    slot_starts = jnp.cumsum(lengths) - lengths
    slot_ends = slot_starts + lengths
    positions = jnp.arange(pool_rows, dtype=jnp.int32)
    owned_rows = (positions[None, :] >= slot_starts[:, None]) & (
        positions[None, :] < slot_ends[:, None]
    )
    owned_rows = owned_rows[:, None, None, :]
    raw_scores = (
        jnp.einsum("rkgc,pkc->rkgp", slot_queries, keys_local, preferred_element_type=jnp.float32)
        * score_scale
    )
    weights = softmax_rounded(jnp.where(owned_rows, raw_scores, masked_score))
    attended = jnp.einsum(
        "rkgp,pkc->rkgc", weights, values_local, preferred_element_type=jnp.float32
    )
    attended = attended.astype(jnp.bfloat16).reshape(rows_dev, kv_local, per_group * head_size)
    spread = lax.all_to_all(attended, "att", split_axis=2, concat_axis=0, tiled=True)
    pieces = lax.all_gather(spread, "ffn", axis=1, tiled=True)
    inverse = (
        jnp.zeros((requests,), jnp.int32).at[assignment].set(jnp.arange(requests, dtype=jnp.int32))
    )
    request_pieces = jnp.take(pieces, inverse, axis=0)
    block = request_pieces
    projected = lax.psum_scatter(
        jnp.einsum("rkc,kcd->rd", block, out_weight, preferred_element_type=jnp.float32).astype(
            jnp.bfloat16
        ),
        "att",
        scatter_dimension=0,
        tiled=True,
    ).astype(jnp.float32)
    middle_short = (hidden_state.astype(jnp.float32) + projected).astype(jnp.bfloat16)
    middle = lax.optimization_barrier(middle_short).astype(jnp.float32)
    squares = lax.psum(jnp.sum(middle * middle, axis=1), "ffn")
    normed = (
        middle * lax.rsqrt(squares[:, None] / model_width + epsilon) * norm_gain.astype(jnp.float32)
    ).astype(jnp.bfloat16)
    every_row = lax.all_gather(normed, "att", axis=0, tiled=True)
    contract = (((1,), (1,)), ((), ()))
    gate_part = lax.dot_general(
        gate_weight, every_row, contract, preferred_element_type=jnp.float32
    )
    up_part = lax.dot_general(up_weight, every_row, contract, preferred_element_type=jnp.float32)
    totals = lax.psum(
        jnp.concatenate([gate_part, up_part], axis=1).astype(jnp.bfloat16), "ffn"
    ).astype(jnp.float32)
    unit_active = (jax.nn.silu(totals[:, :requests]) * totals[:, requests:]).astype(jnp.bfloat16)
    block = unit_active
    returned = lax.psum_scatter(
        lax.dot_general(
            block, down_weight, (((0,), (0,)), ((), ())), preferred_element_type=jnp.float32
        ).astype(jnp.bfloat16),
        "att",
        scatter_dimension=0,
        tiled=True,
    ).astype(jnp.float32)
    return (middle + returned).astype(jnp.bfloat16)


def solution(mesh):
    in_specs = (
        P(("group", "att"), "ffn"),
        P(("group", "att"), "ffn"),
        P(("group", "att"), "ffn"),
        P(("group", "att"), "ffn"),
        P(("group", "att")),
        P("group"),
        P(None, "att", "ffn"),
        P("ffn"),
        P("att", "ffn"),
        P("att", "ffn"),
        P("att", "ffn"),
    )
    out_specs = P(("group", "att"), "ffn")
    return jax.shard_map(
        per_device, mesh=mesh, in_specs=in_specs, out_specs=out_specs, check_vma=False
    )
```

profile of v0, /device:TPU:0, one launch (start us, length us, event | category | flops | bytes accessed | tf_op | source)
XLA Modules:
  0.0 247.6 jit_solution(2298963000983809994)
XLA Ops:
  6.5 0.7 compare_and_fusion
  7.3 16.4 %all-gather = bf16[4,20,2048]{2,1,0:T(8,128)(2,1)S(1)} all-gather(bf16[1,20,2048]{2,1,0:T(8,128)(2,1)} %bitcast.50), channel_id=1, replica_groups=mesh['group'=2,'att'=4,'ffn'=4] {'att'}, dimensions={0}, use_global_device_ids=true | all-gather | bytes 409600 | tf_op jit(solution)/shard_map/all_gather | solution.py:45
  23.7 0.1 reshape.124
  23.8 0.6 gather_fusion
  24.4 0.7 copy.34
  25.2 0.1 reduce
  25.3 0.7 sub.11
  26.0 0.3 fusion.11
  26.3 13.3 %reshape.93 = bf16[12800,2,128]{2,1,0:T(2,128)(2,1)} reshape(bf16[12800,256]{1,0:T(8,128)(2,1)} %param.13) | data formatting | bytes 13107200 | tf_op jit(solution)/shard_map/reshape | solution.py:50
  39.6 13.2 %reshape.94 = bf16[12800,2,128]{2,1,0:T(2,128)(2,1)} reshape(bf16[12800,256]{1,0:T(8,128)(2,1)} %param.14) | data formatting | bytes 13107200 | tf_op jit(solution)/shard_map/reshape | solution.py:51
  52.8 12.1 %fusion.33 = (f32[20,2,8]{2,0,1:T(8,128)S(1)}, f32[20,2,8,12800]{3,2,0,1:T(8,128)}) fusion(bf16[12800,2,128,1]{2,1,0,3:T(2,128)(2,1)} %bitcast.42, pred[20]{0:T(512)(128)(4,1)S(1)} %get-tuple-element.5, pred[20,12800]{1,0:T(8,128)(4,1)S(1)} %fusion.11, bf16[24,16,128]{2,1,0:T(8,128)(2,1)S(1)} %bitcast.46), kind=kOutput, calls=%fused_computation.55 | convolution fusion | flops 1060904640 | bytes 23328512 | tf_op jit(solution)/shard_map/rkgc,pkc->rkgp/dot_general | solution.py:60
  64.9 8.0 %fusion.4 = f32[20,2,8]{2,0,1:T(8,128)S(1)} fusion(f32[20,2,8,12800]{3,2,0,1:T(8,128)} %get-tuple-element.8, f32[20,2,8]{2,0,1:T(8,128)S(1)} %get-tuple-element.7), kind=kLoop, calls=%fused_computation.8 | loop fusion | flops 8191680 | bytes 16386560 | tf_op jit(solution)/shard_map/reduce_sum | solution.py:15
  72.9 10.5 %fusion.16 = bf16[20,2,8,128]{3,2,0,1:T(8,128)(2,1)S(1)} fusion(bf16[12800,2,128,1]{2,1,0,3:T(2,128)(2,1)} %bitcast.43, f32[20,2,8,12800]{3,2,0,1:T(8,128)} %get-tuple-element.8, f32[20,2,8]{2,0,1:T(8,128)S(1)} %fusion.4, f32[20,2,8]{2,0,1:T(8,128)S(1)} %get-tuple-element.7), kind=kOutput, calls=%fused_computation.26 | convolution fusion | flops 1060904960 | bytes 23022080 | tf_op jit(solution)/shard_map/rkgp,pkc->rkgc/dot_general | solution.py:64
  83.3 0.3 copy.54
  83.7 1.6 reshape.136
  85.3 5.6 %all-to-all-start = ((bf16[4,2,5120]{2,1,0:T(2,128)(2,1)}), bf16[4,2,5120]{2,1,0:T(2,128)(2,1)S(1)}, u32[]{:S(2)}, u32[]{:S(2)}) async-start(bf16[4,2,5120]{2,1,0:T(2,128)(2,1)} %reshape.136), calls=%async_computation | async-start | bytes 163840 | tf_op jit(solution)/shard_map/all_to_all | solution.py:68
  90.9 0.8 scatter_custom_fusion
  91.8 4.9 %all-to-all-done = bf16[4,2,5120]{2,1,0:T(2,128)(2,1)S(1)} async-done(((bf16[4,2,5120]{2,1,0:T(2,128)(2,1)}), bf16[4,2,5120]{2,1,0:T(2,128)(2,1)S(1)}, u32[]{:S(2)}, u32[]{:S(2)}) %all-to-all-start) | async-done | bytes 81952 | tf_op jit(solution)/shard_map/all_to_all | solution.py:68
  96.7 1.3 reshape.137
  98.0 0.4 copy.53
  98.4 0.1 copy.41
  98.5 6.1 %all_gather.10 = bf16[80,8,256]{2,0,1:T(8,128)(2,1)S(1)} all-gather(bf16[80,2,256]{2,0,1:T(8,128)(2,1)S(1)} %copy.42), channel_id=1, replica_groups=mesh['group'=2,'att'=4,'ffn'=4] {'ffn'}, dimensions={1}, use_global_device_ids=true | all-gather | bytes 409600 | tf_op jit(solution)/shard_map/all_gather | solution.py:69
  104.6 0.1 copy.43
  104.7 0.6 gather_fusion.1
  105.4 0.2 broadcast_select_fusion
  105.5 4.9 %fusion.10 = bf16[80,2048]{1,0:T(8,128)(2,1)S(1)} fusion(bf16[8,256,2048]{2,1,0:T(8,128)(2,1)} %param.17, bf16[80,8,256]{2,1,0:T(8,128)(2,1)S(1)} %broadcast_select_fusion), kind=kOutput, calls=%fused_computation.18 | convolution fusion | flops 671252480 | bytes 9043968 | tf_op jit(solution)/shard_map/rkc,kcd->rd/dot_general | solution.py:76
  110.5 17.1 %fusion = bf16[24,2048]{1,0:T(8,128)(2,1)S(1)} fusion(bf16[80,2048]{1,0:T(8,128)(2,1)S(1)} %fusion.10), kind=kCustom, calls=%all-reduce-scatter | all-reduce-scatter fusion | flops 196609 | bytes 426496
  127.6 1.3 collective-permute-start
  129.0 0.6 dynamic-slice.6
  130.2 0.6 collective-permute-done
  130.8 0.2 concatenate.5
  131.1 0.1 fusion.22
  131.2 5.7 %psum.14 = f32[20]{0:T(128)S(1)} all-reduce(f32[20]{0:T(128)S(1)} %fusion.22), channel_id=1, replica_groups=mesh['group'=2,'att'=4,'ffn'=4] {'ffn'}, use_global_device_ids=true, to_apply=%region_6.7 | all-reduce | flops 20 | bytes 160 | tf_op jit(solution)/shard_map/psum | solution.py:85
  136.9 0.1 fusion.26
  137.0 14.3 %all-gather.1 = bf16[4,20,2048]{2,1,0:T(8,128)(2,1)S(1)} all-gather(bf16[1,20,2048]{2,1,0:T(8,128)(2,1)S(1)} %fusion.26), channel_id=1, replica_groups=mesh['group'=2,'att'=4,'ffn'=4] {'att'}, dimensions={0}, use_global_device_ids=true | all-gather | bytes 409600 | tf_op jit(solution)/shard_map/all_gather | solution.py:89
  151.3 0.1 reshape.126
  151.4 9.7 %fusion.8 = bf16[3584,80]{0,1:T(8,128)(2,1)S(1)} fusion(bf16[80,2048]{1,0:T(8,128)(2,1)S(1)} %reshape.126, bf16[3584,2048]{1,0:T(8,128)(2,1)} %param.19), kind=kOutput, calls=%fused_computation.14 | convolution fusion | flops 1174691840 | bytes 15581184 | tf_op jit(solution)/shard_map/dot_general | solution.py:91
  161.1 9.7 %fusion.9 = bf16[3584,80]{0,1:T(8,128)(2,1)S(1)} fusion(bf16[80,2048]{1,0:T(8,128)(2,1)S(1)} %reshape.126, bf16[3584,2048]{1,0:T(8,128)(2,1)} %param.20), kind=kOutput, calls=%fused_computation.15 | convolution fusion | flops 1174691840 | bytes 15581184 | tf_op jit(solution)/shard_map/dot_general | solution.py:94
  170.9 1.1 pad_maximum_fusion
  172.0 0.0 all-reduce.6.cloned.1.call-update
  172.0 38.0 %all-reduce.6.cloned.1.call-done = bf16[3584,160]{0,1:T(8,128)(2,1)} async-done(((bf16[3584,160]{0,1:T(8,128)(2,1)}), bf16[3584,160]{0,1:T(8,128)(2,1)}) %all-reduce.6.cloned.1.call-update) | async-done | bytes 1146896 | tf_op jit(solution)/shard_map/psum | solution.py:95
  210.1 1.5 convert_element_type.56
  211.6 7.9 %convolution_convert_fusion.2 = bf16[80,2048]{1,0:T(8,128)(2,1)S(1)} fusion(bf16[3584,2048]{1,0:T(8,128)(2,1)} %param.21, f32[3584,160]{0,1:T(8,128)S(1)} %convert_element_type.56), kind=kOutput, calls=%fused_computation.17 | convolution fusion | flops 1176289280 | bytes 17301504 | tf_op jit(solution)/shard_map/dot_general | solution.py:101
  219.5 15.8 %fusion.1 = bf16[24,2048]{1,0:T(8,128)(2,1)S(1)} fusion(bf16[80,2048]{1,0:T(8,128)(2,1)S(1)} %convolution_convert_fusion.2), kind=kCustom, calls=%all-reduce-scatter.1 | all-reduce-scatter fusion | flops 196609 | bytes 426496
  235.3 2.7 %collective-permute-start.1 = (bf16[12,2048]{1,0:T(8,128)(2,1)S(1)}, bf16[12,2048]{1,0:T(8,128)(2,1)S(1)}, u32[]{:S(2)}, u32[]{:S(2)}) collective-permute-start(bf16[12,2048]{1,0:T(8,128)(2,1)S(1)} %slice.15), channel_id=1, source_target_pairs={{0,4},{4,8},{8,12},{1,5},{5,9},{9,13},{2,6},{6,10},{10,14},{3,7},{... | collective-permute-start | bytes 147464
  238.0 1.9 collective-permute-done.1
  239.9 0.2 concatenate.6
  240.1 0.7 fusion.25
  (23 shorter events, 0.2 us)
Async XLA Ops:
  72.9 18.0 %copy-start.3 = (s32[80]{0:T(128)S(1)}, s32[80]{0:T(128)}, u32[]{:S(2)}) copy-start(s32[80]{0:T(128)} %param.16) | copy-start | bytes 964
  85.3 11.3 %all-to-all-start = ((bf16[4,2,5120]{2,1,0:T(2,128)(2,1)}), bf16[4,2,5120]{2,1,0:T(2,128)(2,1)S(1)}, u32[]{:S(2)}, u32[]{:S(2)}) async-start(bf16[4,2,5120]{2,1,0:T(2,128)(2,1)} %reshape.136), calls=%async_computation | async-start | bytes 163840 | tf_op jit(solution)/shard_map/all_to_all | solution.py:68
  90.9 119.2 %all-reduce.6.cloned.1.call-start = ((), (), s32[]{:S(2)}) async-start(), calls=%async_computation.1 | async-start | bytes 2293760 | tf_op jit(solution)/shard_map/psum | solution.py:95
  104.7 24.2 %copy-start.1 = (bf16[2048]{0:T(1024)(128)(2,1)S(1)}, bf16[2048]{0:T(1024)(128)(2,1)}, u32[]{:S(2)}) copy-start(bf16[2048]{0:T(1024)(128)(2,1)} %param.18) | copy-start | bytes 12292
  104.7 24.2 %copy-start.2 = (u32[32]{0:T(128)S(1)}, u32[32]{0:T(128)}, u32[]{:S(2)}) copy-start(u32[32]{0:T(128)} %constant.63) | copy-start | bytes 388
  105.4 25.7 %copy-start = (bf16[20,2048]{1,0:T(8,128)(2,1)S(1)}, bf16[20,2048]{1,0:T(8,128)(2,1)}, u32[]{:S(2)}) copy-start(bf16[20,2048]{1,0:T(8,128)(2,1)} %param.11) | copy-start | bytes 245764
  127.6 3.2 %collective-permute-start = (bf16[12,2048]{1,0:T(8,128)(2,1)S(1)}, bf16[12,2048]{1,0:T(8,128)(2,1)S(1)}, u32[]{:S(2)}, u32[]{:S(2)}) collective-permute-start(bf16[12,2048]{1,0:T(8,128)(2,1)S(1)} %slice.14), channel_id=1, source_target_pairs={{0,4},{4,8},{8,12},{1,5},{5,9},{9,13},{2,6},{6,10},{10,14},{3,7},{... | collective-permute-start | bytes 147464
  235.3 4.6 %collective-permute-start.1 = (bf16[12,2048]{1,0:T(8,128)(2,1)S(1)}, bf16[12,2048]{1,0:T(8,128)(2,1)S(1)}, u32[]{:S(2)}, u32[]{:S(2)}) collective-permute-start(bf16[12,2048]{1,0:T(8,128)(2,1)S(1)} %slice.15), channel_id=1, source_target_pairs={{0,4},{4,8},{8,12},{1,5},{5,9},{9,13},{2,6},{6,10},{10,14},{3,7},{... | collective-permute-start | bytes 147464
Sparse Core Ops, SparseCore 0:
  172.1 37.8 all-reduce.5
where the time goes:
time: 249 us; the launch traced here: 248 us
  blocking collectives  75.4 us (30%)
  matrix products  54.8 us (22%)
  waiting for transfers between devices  45.4 us (18%)
  local copies, waits for them, and re-layouts  34.4 us (14%)
  between operations  14.3 us (6%)
  other arithmetic  13.6 us (5%)
  starting transfers between devices  9.56 us (4%)
    psum x1, waiting for transfers between devices, per_device(): lax.psum(jnp.concatenate([gate_part, up_part], axis=1).astype(jnp.bfloat1...  38 us
    unnamed x2, blocking collectives  32.9 us
    all_gather x1, blocking collectives, per_device(): every_query = lax.all_gather(queries, 'att', axis=0, tiled=True)  16.4 us
    all_gather x1, blocking collectives, per_device(): every_row = lax.all_gather(normed, 'att', axis=0, tiled=True)  14.3 us
    reshape x1, local copies, waits for them, and re-layouts, per_device(): keys_local = key_cache.reshape(pool_rows, kv_local, head_size)  13.3 us
    reshape x1, local copies, waits for them, and re-layouts, per_device(): values_local = value_cache.reshape(pool_rows, kv_local, head_size)  13.2 us
    dot_general x1, matrix products, per_device(): jnp.einsum('rkgc,pkc->rkgp', slot_queries, keys_local, preferred_element_...  12.1 us
    dot_general x1, matrix products, per_device(): jnp.einsum('rkgp,pkc->rkgc', weights, values_local, preferred_element_typ...  10.5 us
  transfers between devices with their start and end apart: 4, of which 4 were waited for; matrix products, arithmetic and copies ran while one was open for 1% of the time, Pallas kernels for 0%

commit v1 on v0

--- a/solution.py
+++ b/solution.py
@@ -1,8 +1,11 @@
+import functools
 import math
 
 import jax
 import jax.numpy as jnp
 from jax import lax
+from jax.experimental import pallas as pl
+from jax.experimental.pallas import tpu as pltpu
 from jax.sharding import PartitionSpec as P
 
 epsilon = 1e-05
@@ -44,12 +47,14 @@
     att_place = lax.axis_index("att")
     every_query = lax.all_gather(queries, "att", axis=0, tiled=True)
     own_slots = lax.dynamic_slice_in_dim(assignment, att_place * rows_dev, rows_dev)
-    slot_queries = jnp.take(every_query, own_slots, axis=0).reshape(
+    chosen = (own_slots[:, None] == jnp.arange(requests, dtype=jnp.int32)).astype(jnp.bfloat16)
+    slot_queries = (chosen @ every_query).reshape(
         rows_dev, kv_local, per_group, head_size
     )
     keys_local = key_cache.reshape(pool_rows, kv_local, head_size)
     values_local = value_cache.reshape(pool_rows, kv_local, head_size)
-    slot_starts = jnp.cumsum(lengths) - lengths
+    slots = jnp.arange(rows_dev, dtype=jnp.int32)
+    slot_starts = jnp.sum(jnp.where(slots[None, :] < slots[:, None], lengths[None, :], 0), axis=1)
     slot_ends = slot_starts + lengths
     positions = jnp.arange(pool_rows, dtype=jnp.int32)
     owned_rows = (positions[None, :] >= slot_starts[:, None]) & (
@@ -67,10 +72,8 @@
     attended = attended.astype(jnp.bfloat16).reshape(rows_dev, kv_local, per_group * head_size)
     spread = lax.all_to_all(attended, "att", split_axis=2, concat_axis=0, tiled=True)
     pieces = lax.all_gather(spread, "ffn", axis=1, tiled=True)
-    inverse = (
-        jnp.zeros((requests,), jnp.int32).at[assignment].set(jnp.arange(requests, dtype=jnp.int32))
-    )
-    request_pieces = jnp.take(pieces, inverse, axis=0)
+    placed = (jnp.arange(requests, dtype=jnp.int32)[:, None] == assignment).astype(jnp.bfloat16)
+    request_pieces = (placed @ pieces.reshape(requests, -1)).reshape(pieces.shape)
     block = request_pieces
     projected = lax.psum_scatter(
         jnp.einsum("rkc,kcd->rd", block, out_weight, preferred_element_type=jnp.float32).astype(
@@ -108,6 +111,534 @@
     return (middle + returned).astype(jnp.bfloat16)
 
 
+MESH = pl.DeviceIdType.MESH
+NT = (((1,), (1,)), ((), ()))
+
+
+def flip(index, bits):
+    result, bit = index, 1
+    while bit <= bits:
+        if bits & bit:
+            result = result + bit - 2 * bit * ((index // bit) % 2)
+        bit *= 2
+    return result
+
+
+def tile_of(total, most):
+    tile = most - most % 128
+    while total % tile:
+        tile -= 128
+    return tile
+
+
+def one_hot(targets, width):
+    lanes = lax.broadcasted_iota(jnp.int32, (targets.shape[0], width), 1)
+    return (lanes == targets).astype(jnp.bfloat16)
+
+
+def pick(targets, table):
+    return jnp.dot(
+        one_hot(targets, table.shape[0]), table, preferred_element_type=jnp.float32
+    ).astype(jnp.bfloat16)
+
+
+def layer_kernel(
+    sizes,
+    places,
+    query_ref,
+    hidden_ref,
+    gain_ref,
+    index_ref,
+    key_hbm,
+    value_hbm,
+    out_hbm,
+    gate_hbm,
+    up_hbm,
+    down_hbm,
+    result_ref,
+    keys,
+    values,
+    out_w,
+    gate_w,
+    up_w,
+    every_query,
+    spread_out,
+    spread_in,
+    pieces,
+    blocks,
+    part_out,
+    part_in,
+    middle,
+    every_row,
+    rows,
+    sq_own,
+    sq_in,
+    sq_total,
+    sq_all,
+    gu_out,
+    gu_in,
+    active,
+    load_sem,
+    gu_load_sem,
+    down_sem,
+    att_send,
+    att_recv,
+    ffn_send,
+    ffn_recv,
+    part_send,
+    part_recv,
+    last_send,
+    last_recv,
+):
+    n_att, n_ffn, rows_dev, pad, kv_local, per_group, head = sizes
+    att = lax.axis_index("att")
+    ffn = lax.axis_index("ffn")
+    requests = n_att * rows_dev
+    columns = out_w.shape[1]
+    model_width = columns * n_ffn
+    units = gate_w.shape[0] // n_ffn
+    bf16, f32 = jnp.bfloat16, jnp.float32
+
+    def ix(name):
+        at, count = places[name]
+        return index_ref[:count, at : at + 1]
+
+    key_load = pltpu.make_async_copy(key_hbm, keys, load_sem.at[0])
+    value_load = pltpu.make_async_copy(value_hbm, values, load_sem.at[1])
+    key_load.start()
+    value_load.start()
+    kv_total, group_rows = out_hbm.shape[0], out_hbm.shape[1]
+    out_loads = [
+        pltpu.make_async_copy(
+            out_hbm.at[k], out_w.at[pl.ds(k * group_rows, group_rows), :], load_sem.at[2 + k]
+        )
+        for k in range(kv_total)
+    ]
+    for copy in out_loads:
+        copy.start()
+    order = list(range(n_ffn - 1, -1, -1))
+    unit_rows = [pl.ds(pl.multiple_of(flip(ffn, d) * units, units), units) for d in range(n_ffn)]
+    gu_loads = {}
+    for d in order:
+        gu_loads[d] = [
+            pltpu.make_async_copy(
+                source.at[unit_rows[d], :], target.at[unit_rows[d], :], gu_load_sem.at[n, d]
+            )
+            for n, (source, target) in enumerate(((gate_hbm, gate_w), (up_hbm, up_w)))
+        ]
+        for copy in gu_loads[d]:
+            copy.start()
+
+    att_peer = [lax.rem(att + d, n_att) for d in range(n_att)]
+    ffn_peer = [flip(ffn, d) for d in range(n_ffn)]
+    barrier = pltpu.get_barrier_semaphore()
+    for d in range(1, n_att):
+        pl.semaphore_signal(barrier, inc=1, device_id={"att": att_peer[d]}, device_id_type=MESH)
+    for d in range(1, n_ffn):
+        pl.semaphore_signal(barrier, inc=1, device_id={"ffn": ffn_peer[d]}, device_id_type=MESH)
+    pl.semaphore_wait(barrier, n_att + n_ffn - 2)
+
+    def to_att(phase, d, source, target):
+        copy = pltpu.make_async_remote_copy(
+            src_ref=source,
+            dst_ref=target,
+            send_sem=att_send.at[phase, d - 1],
+            recv_sem=att_recv.at[phase, d - 1],
+            device_id={"att": att_peer[d]},
+            device_id_type=MESH,
+        )
+        copy.start()
+        return copy
+
+    def to_ffn(phase, d, source, target):
+        copy = pltpu.make_async_remote_copy(
+            src_ref=source,
+            dst_ref=target,
+            send_sem=ffn_send.at[phase, d - 1],
+            recv_sem=ffn_recv.at[phase, d - 1],
+            device_id={"ffn": ffn_peer[d]},
+            device_id_type=MESH,
+        )
+        copy.start()
+        return copy
+
+    sent = []
+    every_query_copies = [
+        to_att(0, d, query_ref, every_query.at[att]) for d in range(1, n_att)
+    ]
+    every_query[pl.ds(att, 1)] = query_ref[...][None]
+    for copy in every_query_copies:
+        copy.wait()
+    query_table = every_query[...].reshape(-1, head)
+    slot_rows = rows_dev * per_group
+    query_at = ix("query")
+    slot_query = [
+        pick(query_at[k * slot_rows : (k + 1) * slot_rows], query_table) for k in range(kv_local)
+    ]
+
+    first, count = ix("first"), ix("count")
+    pool = keys.shape[0]
+    block = tile_of(pool, 512)
+    scale = 1.0 / math.sqrt(head)
+    key_load.wait()
+    value_load.wait()
+
+    def attend(step, carry):
+        at = pl.multiple_of(step * block, block)
+        spot = lax.broadcasted_iota(jnp.int32, (slot_rows, block), 1) + (at - first)
+        owned = (spot >= 0) & (spot < count)
+        new = []
+        for k in range(kv_local):
+            top, total, out = carry[k]
+            lanes = slice(k * head, (k + 1) * head)
+            scores = lax.dot_general(
+                slot_query[k],
+                keys[pl.ds(at, block), lanes],
+                NT,
+                preferred_element_type=f32,
+            )
+            scores = jnp.where(owned, scores * scale, -1e30)
+            new_top = jnp.maximum(top, jnp.max(scores, axis=1, keepdims=True))
+            shifted = jnp.where(owned, jnp.exp(scores - new_top), 0.0)
+            keep = jnp.exp(top - new_top)
+            total = total * keep + jnp.sum(shifted, axis=1, keepdims=True)
+            out = out * keep + jnp.dot(
+                shifted.astype(bf16), values[pl.ds(at, block), lanes], preferred_element_type=f32
+            )
+            new.append((new_top, total, out))
+        return tuple(new)
+
+    start = tuple(
+        (
+            jnp.full((slot_rows, 1), -1e30, f32),
+            jnp.zeros((slot_rows, 1), f32),
+            jnp.zeros((slot_rows, head), f32),
+        )
+        for _ in range(kv_local)
+    )
+    finished = lax.fori_loop(0, pool // block, attend, start)
+    attended = jnp.concatenate([(out / total).astype(bf16) for _, total, out in finished], axis=0)
+
+    spread_out[...] = pick(ix("spread"), attended).reshape(spread_out.shape)
+    spread_copies = [
+        to_att(1, d, spread_out.at[att_peer[d]], spread_in.at[att]) for d in range(1, n_att)
+    ]
+    spread_in[pl.ds(att, 1)] = spread_out[pl.ds(att, 1)]
+    for copy in spread_copies:
+        copy.wait()
+    piece_copies = [to_ffn(0, d, spread_in, pieces.at[ffn]) for d in range(1, n_ffn)]
+    pieces[pl.ds(ffn, 1)] = spread_in[...][None]
+    for copy in piece_copies:
+        copy.wait()
+
+    table = jnp.concatenate(
+        [pieces[f].reshape(-1, head) for f in range(n_ffn)], axis=1
+    )
+    padded = n_att * pad
+    request_at = ix("request")
+    parts_kv = request_at.shape[0] // padded
+    for n in range(parts_kv):
+        picked = pick(request_at[n * padded : (n + 1) * padded], table)
+        for f in range(n_ffn):
+            at = (f * parts_kv + n) * head
+            blocks[:, at : at + head] = picked[:, f * head : (f + 1) * head]
+    for copy in out_loads:
+        copy.wait()
+
+    wide = tile_of(columns, 512)
+    chunks = columns // wide
+
+    def to_owner(c, d, out_buf, in_buf, send, recv):
+        lanes = pl.ds(c * wide, wide)
+        copy = pltpu.make_async_remote_copy(
+            src_ref=out_buf.at[att_peer[d], :, lanes],
+            dst_ref=in_buf.at[d - 1, :, lanes],
+            send_sem=send.at[d - 1, c],
+            recv_sem=recv.at[d - 1, c],
+            device_id={"att": att_peer[d]},
+            device_id_type=MESH,
+        )
+        copy.start()
+        return copy
+
+    owner_copies = []
+    for c in range(chunks):
+        lanes = slice(c * wide, (c + 1) * wide)
+        product = jnp.dot(blocks[...], out_w[:, lanes], preferred_element_type=f32)
+        part_out[:, :, lanes] = product.astype(bf16).reshape(n_att, pad, wide)
+        owner_copies.append(
+            [to_owner(c, d, part_out, part_in, part_send, part_recv) for d in range(1, n_att)]
+        )
+    squares = jnp.zeros((pad, 1), f32)
+    for c in range(chunks):
+        lanes = slice(c * wide, (c + 1) * wide)
+        for copy in owner_copies[c]:
+            copy.wait()
+        projected = part_out[pl.ds(att, 1), :, lanes].reshape(pad, wide).astype(f32)
+        for d in range(1, n_att):
+            projected = projected + part_in[d - 1, :, lanes].astype(f32)
+        mid_short = (hidden_ref[:, lanes].astype(f32) + projected).astype(bf16)
+        middle[:, lanes] = mid_short
+        mid = mid_short.astype(f32)
+        squares = squares + jnp.sum(mid * mid, axis=1, keepdims=True)
+        every_row[pl.ds(att, 1), :, lanes] = (
+            (mid * gain_ref[:, lanes].astype(f32)).astype(bf16)[None]
+        )
+    row_copies = [
+        to_att(2, d, every_row.at[att], every_row.at[att]) for d in range(1, n_att)
+    ]
+    sq_own[...] = jnp.broadcast_to(squares, sq_own.shape)
+    sq_copies = [to_ffn(1, d, sq_own, sq_in.at[d - 1]) for d in range(1, n_ffn)]
+    for copy in sq_copies:
+        copy.wait()
+    whole = sq_own[...]
+    for d in range(1, n_ffn):
+        whole = whole + sq_in[d - 1]
+    sq_total[...] = lax.rsqrt(whole / model_width + epsilon)
+    sq_all[pl.ds(att, 1)] = sq_total[...][None]
+    scale_copies = [to_att(3, d, sq_total, sq_all.at[att]) for d in range(1, n_att)]
+    for copy in row_copies:
+        copy.wait()
+    row_pick = one_hot(ix("narrow"), padded)
+    for c in range(chunks):
+        lanes = slice(c * wide, (c + 1) * wide)
+        rows[:, lanes] = jnp.dot(
+            row_pick, every_row[:, :, lanes].reshape(padded, wide), preferred_element_type=f32
+        ).astype(bf16)
+
+    gu_copies = []
+    down_loads = []
+    own = None
+    for d in order:
+        for copy in gu_loads[d]:
+            copy.wait()
+        made = []
+        for weight in (gate_w, up_w):
+            total = jnp.zeros((requests, units), f32)
+            for c in range(chunks):
+                lanes = slice(c * wide, (c + 1) * wide)
+                total = total + lax.dot_general(
+                    rows[:, lanes], weight[unit_rows[d], lanes], NT, preferred_element_type=f32
+                )
+            made.append(total)
+        if d:
+            gu_out[d - 1, 0] = made[0].astype(bf16)
+            gu_out[d - 1, 1] = made[1].astype(bf16)
+            gu_copies.append(to_ffn(2, d, gu_out.at[d - 1], gu_in.at[d - 1]))
+        else:
+            own = made
+        load = pltpu.make_async_copy(
+            down_hbm.at[unit_rows[d], :], gate_w.at[unit_rows[d], :], down_sem.at[d]
+        )
+        load.start()
+        down_loads.append(load)
+    for copy in scale_copies:
+        copy.wait()
+    row_scale = jnp.dot(
+        row_pick.astype(f32),
+        sq_all[...].reshape(padded, sq_all.shape[2]),
+        preferred_element_type=f32,
+        precision=lax.Precision.HIGHEST,
+    )[:, :1]
+    gate, upward = own
+    for copy in gu_copies:
+        copy.wait()
+    for d in range(1, n_ffn):
+        gate = gate + gu_in[d - 1, 0].astype(f32)
+        upward = upward + gu_in[d - 1, 1].astype(f32)
+    gate = gate * row_scale
+    unit_active = (gate / (1.0 + jnp.exp(-gate)) * (upward * row_scale)).astype(bf16)
+    active[pl.ds(ffn, 1)] = unit_active[None]
+    active_copies = [
+        to_ffn(3, d, active.at[ffn], active.at[ffn]) for d in range(1, n_ffn)
+    ]
+    for copy in active_copies:
+        copy.wait()
+    widen = one_hot(ix("widen"), requests)
+    for load in down_loads:
+        load.wait()
+
+    last_copies = []
+    for c in range(chunks):
+        lanes = slice(c * wide, (c + 1) * wide)
+        product = jnp.dot(active[0], gate_w[:units, lanes], preferred_element_type=f32)
+        for f in range(1, n_ffn):
+            product = product + jnp.dot(
+                active[f], gate_w[f * units : (f + 1) * units, lanes], preferred_element_type=f32
+            )
+        product = jnp.dot(widen, product.astype(bf16), preferred_element_type=f32)
+        part_out[:, :, lanes] = product.astype(bf16).reshape(n_att, pad, wide)
+        last_copies.append(
+            [to_owner(c, d, part_out, part_in, last_send, last_recv) for d in range(1, n_att)]
+        )
+    for c in range(chunks):
+        lanes = slice(c * wide, (c + 1) * wide)
+        for copy in last_copies[c]:
+            copy.wait()
+        returned = part_out[pl.ds(att, 1), :, lanes].reshape(pad, wide).astype(f32)
+        for d in range(1, n_att):
+            returned = returned + part_in[d - 1, :, lanes].astype(f32)
+        result_ref[:, lanes] = (middle[:, lanes].astype(f32) + returned).astype(bf16)
+
+
+def fused_device(
+    hidden_state,
+    queries,
+    key_cache,
+    value_cache,
+    lengths,
+    assignment,
+    out_weight,
+    norm_gain,
+    gate_weight,
+    up_weight,
+    down_weight,
+):
+    rows_dev, columns = hidden_state.shape
+    n_att, n_ffn = lax.axis_size("att"), lax.axis_size("ffn")
+    requests = rows_dev * n_att
+    kv_total, group_rows, _ = out_weight.shape
+    kv_local = kv_total // n_ffn
+    head = key_cache.shape[1] // kv_local
+    per_group = queries.shape[1] // (kv_local * head)
+    heads_here = group_rows // head
+    pool = key_cache.shape[0]
+    hidden_units = gate_weight.shape[0]
+    units = hidden_units // n_ffn
+    pad = -(-rows_dev // 16) * 16
+    padded = n_att * pad
+    i32, bf16, f32 = jnp.int32, jnp.bfloat16, jnp.float32
+
+    own_slots = lax.dynamic_slice_in_dim(assignment, lax.axis_index("att") * rows_dev, rows_dev)
+    k_ix = jnp.arange(kv_local, dtype=i32)
+    g_ix = jnp.arange(per_group, dtype=i32)
+    s_ix = jnp.arange(rows_dev, dtype=i32)
+    a_ix = jnp.arange(n_att, dtype=i32)
+    h_ix = jnp.arange(heads_here, dtype=i32)
+    query_at = (
+        own_slots[None, :, None] * (kv_local * per_group)
+        + k_ix[:, None, None] * per_group
+        + g_ix[None, None, :]
+    ).reshape(-1)
+    starts = jnp.sum(jnp.where(s_ix[None, :] < s_ix[:, None], lengths[None, :], 0), axis=1)
+    first = jnp.repeat(starts, per_group)
+    count = jnp.repeat(lengths, per_group)
+    spread_at = (
+        k_ix[None, :, None, None] * (rows_dev * per_group)
+        + s_ix[None, None, None, :] * per_group
+        + a_ix[:, None, None, None] * heads_here
+        + h_ix[None, None, :, None]
+    ).reshape(-1)
+    all_ix = jnp.arange(requests, dtype=i32)
+    inverse = jnp.sum(
+        jnp.where(assignment[None, :] == all_ix[:, None], all_ix[None, :], 0), axis=1
+    )
+    inverse_pad = jnp.pad(
+        inverse.reshape(n_att, rows_dev), ((0, 0), (0, pad - rows_dev)), constant_values=-1
+    ).reshape(-1)
+    slot_at = (inverse_pad // rows_dev) * (kv_local * heads_here * rows_dev) + inverse_pad % rows_dev
+    parts = jnp.arange(kv_local * heads_here, dtype=i32)
+    request_at = jnp.where(
+        inverse_pad[None, :] >= 0, slot_at[None, :] + parts[:, None] * rows_dev, -1
+    ).reshape(-1)
+    narrow_at = (a_ix[:, None] * pad + s_ix[None, :]).reshape(-1)
+    p_ix = jnp.arange(pad, dtype=i32)
+    widen_at = jnp.where(
+        p_ix[None, :] < rows_dev, a_ix[:, None] * rows_dev + p_ix[None, :], -1
+    ).reshape(-1)
+    named = [
+        ("query", query_at),
+        ("first", first),
+        ("count", count),
+        ("spread", spread_at),
+        ("request", request_at),
+        ("narrow", narrow_at),
+        ("widen", widen_at),
+    ]
+    longest = max(array.shape[0] for _, array in named)
+    places = {name: (n, array.shape[0]) for n, (name, array) in enumerate(named)}
+    index = jnp.stack([jnp.pad(array, (0, longest - array.shape[0])) for _, array in named], axis=1)
+
+    query_rows = queries.reshape(-1, head)
+    hidden_pad = jnp.pad(hidden_state, ((0, pad - rows_dev), (0, 0)))
+    piece_rows = kv_local * heads_here * rows_dev
+    wide = tile_of(columns, 512)
+    chunks = columns // wide
+    sizes = (n_att, n_ffn, rows_dev, pad, kv_local, per_group, head)
+    vmem = pl.BlockSpec(memory_space=pltpu.VMEM)
+    hbm = pl.BlockSpec(memory_space=pl.ANY)
+    dma = pltpu.SemaphoreType.DMA
+    V = pltpu.VMEM
+    flops = 2 * requests * columns * (3 * hidden_units + kv_total * group_rows)
+    moved = 2 * columns * (3 * hidden_units + kv_total * group_rows) + 4 * key_cache.size
+    result = pl.pallas_call(
+        functools.partial(layer_kernel, sizes, places),
+        out_shape=jax.ShapeDtypeStruct((pad, columns), bf16),
+        in_specs=[vmem] * 4 + [hbm] * 6,
+        out_specs=vmem,
+        scratch_shapes=[
+            V(key_cache.shape, bf16),
+            V(value_cache.shape, bf16),
+            V((kv_total * group_rows, columns), bf16),
+            V(gate_weight.shape, bf16),
+            V(up_weight.shape, bf16),
+            V((n_att,) + query_rows.shape, bf16),
+            V((n_att, piece_rows, head), bf16),
+            V((n_att, piece_rows, head), bf16),
+            V((n_ffn, n_att, piece_rows, head), bf16),
+            V((padded, kv_total * group_rows), bf16),
+            V((n_att, pad, columns), bf16),
+            V((n_att - 1, pad, columns), bf16),
+            V((pad, columns), bf16),
+            V((n_att, pad, columns), bf16),
+            V((requests, columns), bf16),
+            V((pad, 128), f32),
+            V((n_ffn - 1, pad, 128), f32),
+            V((pad, 128), f32),
+            V((n_att, pad, 128), f32),
+            V((n_ffn - 1, 2, requests, units), bf16),
+            V((n_ffn - 1, 2, requests, units), bf16),
+            V((n_ffn, requests, units), bf16),
+            dma((2 + kv_total,)),
+            dma((2, n_ffn)),
+            dma((n_ffn,)),
+            dma((4, n_att - 1)),
+            dma((4, n_att - 1)),
+            dma((4, n_ffn - 1)),
+            dma((4, n_ffn - 1)),
+            dma((n_att - 1, chunks)),
+            dma((n_att - 1, chunks)),
+            dma((n_att - 1, chunks)),
+            dma((n_att - 1, chunks)),
+        ],
+        compiler_params=pltpu.CompilerParams(
+            collective_id=0, has_side_effects=True, vmem_limit_bytes=61 * 2**20
+        ),
+        cost_estimate=pl.CostEstimate(flops=flops, bytes_accessed=moved, transcendentals=0),
+        name="decode_layer",
+    )(
+        query_rows,
+        hidden_pad,
+        norm_gain[None, :],
+        index,
+        key_cache,
+        value_cache,
+        out_weight,
+        gate_weight,
+        up_weight,
+        down_weight,
+    )
+    return result[:rows_dev]
+
+
+def fits_kernel(mesh, out_weight, key_cache, gate_weight):
+    n_att, n_ffn = mesh.shape["att"], mesh.shape["ffn"]
+    head = key_cache.shape[1] // out_weight.shape[0]
+    group_rows = out_weight.shape[1] // n_att
+    units = gate_weight.shape[0] // (n_att * n_ffn)
+    return n_ffn & (n_ffn - 1) == 0 and group_rows % head == 0 and units % 128 == 0
+
+
 def solution(mesh):
     in_specs = (
         P(("group", "att"), "ffn"),
@@ -123,6 +654,11 @@
         P("att", "ffn"),
     )
     out_specs = P(("group", "att"), "ffn")
-    return jax.shard_map(
-        per_device, mesh=mesh, in_specs=in_specs, out_specs=out_specs, check_vma=False
-    )
+
+    def run(*arrays):
+        body = fused_device if fits_kernel(mesh, arrays[6], arrays[2], arrays[8]) else per_device
+        return jax.shard_map(
+            body, mesh=mesh, in_specs=in_specs, out_specs=out_specs, check_vma=False
+        )(*arrays)
+
+    return run

time: 249 us -> 118 us (0.47)
  Pallas kernels: 0 us -> 105 us
  blocking collectives: 75.4 us -> 0 us
  matrix products: 54.8 us -> 0 us
  waiting for transfers between devices: 45.4 us -> 0 us
  local copies, waits for them, and re-layouts: 34.4 us -> 8.64 us
  between operations: 14.3 us -> 0.1 us
  other arithmetic: 13.6 us -> 2.83 us
  starting transfers between devices: 9.56 us -> 0 us
    pallas_call x0 -> x1, Pallas kernels: none -> 105 us  [fused_device(): pl.pallas_call(functools.partial(layer_kernel, sizes, places), out_shape=...]
    dot_general x6 -> x0, matrix products: 54.8 us -> none  [the longest x1 12.1 us: per_device(): jnp.einsum('rkgc,pkc->rkgp', slot_queries, keys_local, preferred_element_...]
    psum x1 -> x0, waiting for transfers between devices: 38 us -> none  [per_device(): lax.psum(jnp.concatenate([gate_part, up_part], axis=1).astype(jnp.bfloat1...]
    all_gather x3 -> x0, blocking collectives: 36.9 us -> none  [the longest x1 16.4 us: per_device(): every_query = lax.all_gather(queries, 'att', axis=0, tiled=True)]
    unnamed x2 -> x0, blocking collectives: 32.9 us -> none
    reshape x3 -> x4, local copies, waits for them, and re-layouts: 26.8 us -> 1.85 us  [the longest x1 1.59 us: fused_device(): query_rows = queries.reshape(-1, head)]
    reduce_sum x2, other arithmetic: 8.09 us -> 1.53 us  [the longest x1 0.77 us: fused_device(): jnp.sum(jnp.where(s_ix[None, :] < s_ix[:, None], lengths[None, :], 0), ax...]
    psum x1 -> x0, blocking collectives: 5.66 us -> none  [per_device(): squares = lax.psum(jnp.sum(middle * middle, axis=1), 'ffn')]
  transfers between devices with their start and end apart: 4 -> 0, of which waited for: 4 -> 0; matrix products, arithmetic and copies ran while one was open for 1% -> 0% of each run, Pallas kernels for 0% -> 0%
where the time goes in v1:
time: 118 us; the launch traced here: 117 us
  Pallas kernels  105 us (89%)
  local copies, waits for them, and re-layouts  8.64 us (7%)
  other arithmetic  2.83 us (2%)
    pallas_call x1, Pallas kernels, fused_device(): pl.pallas_call(functools.partial(layer_kernel, sizes, places), out_shape=...  105 us

profile of v1, /device:TPU:0, one launch (start us, length us, event | category | flops | bytes accessed | tf_op | source)
XLA Modules:
  0.0 117.0 jit_solution(4747377615357221541)
XLA Ops:
  0.0 0.7 dynamic-slice_multiply_fusion
  0.7 0.8 select_reduce_fusion.1
  1.5 0.8 select_reduce_fusion
  2.3 0.1 broadcast_add_fusion.2
  2.4 0.1 broadcast_add_fusion.1
  2.5 0.1 reshape.221
  2.6 0.1 ge.18
  2.6 0.1 ne.38
  2.7 0.1 add_select_fusion
  2.8 0.1 select_n.61
  2.9 0.1 iota_add_fusion.2
  3.0 0.1 add.208
  3.1 0.1 div.14
  3.2 0.1 rem.24
  3.2 0.1 add_select_fusion.1
  3.3 0.1 broadcast_add_fusion
  3.4 0.1 add.199
  3.5 1.3 %broadcast_in_dim.48.gain_ref = bf16[1,2048]{1,0:T(2,128)(2,1)} reshape(bf16[2048]{0:T(1024)(128)(2,1)} %param.18) | data formatting | bytes 8192 | tf_op jit(solution)/shard_map/broadcast_in_dim | solution.py:622
  4.8 0.1 broadcast_in_dim.78
  4.9 0.1 reshape.219
  5.0 0.7 broadcast_in_dim.79
  5.7 0.1 reshape.220
  5.8 0.1 iota_add_fusion
  5.9 0.1 add.189
  6.0 1.6 %reshape.218.query_ref = bf16[320,128]{1,0:T(8,128)(2,1)} reshape(bf16[20,2048]{1,0:T(8,128)(2,1)} %param.12) | data formatting | bytes 163840 | tf_op jit(solution)/shard_map/reshape | solution.py:562
  7.6 1.6 %pad.30.hidden_ref = bf16[32,2048]{1,0:T(8,128)(2,1)} pad(bf16[20,2048]{1,0:T(8,128)(2,1)} %param.11, bf16[]{:T(256)} %constant.13.clone.1), padding=0_12x0_0 | pad | bytes 212994 | tf_op jit(solution)/shard_map/jit(_pad)/pad | solution.py:563
  9.2 0.8 copy.20.index_ref
  10.0 105.4 %decode_layer.1 = bf16[32,2048]{1,0:T(8,128)(2,1)} custom-call(bf16[320,128]{1,0:T(8,128)(2,1)} %reshape.218.query_ref, bf16[32,2048]{1,0:T(8,128)(2,1)} %pad.30.hidden_ref, bf16[1,2048]{1,0:T(2,128)(2,1)} %broadcast_in_dim.48.gain_ref, s32[512,7]{1,0:T(8,128)} %copy.20.index_ref, bf16[12800,256]{1,0:T(8,128)(2,1)} %key_hbm.1, bf16[12800,256]{1,0:T(8,128)(2,1)} %value_hbm.1, ...), custom_call_target="tpu_custom_call" | custom-call | flops 4194304000 | bytes 65536000 | tf_op jit(solution)/shard_map/decode_layer/pallas_call | solution.py:574
  115.5 1.5 %slice.3 = bf16[20,2048]{1,0:T(8,128)(2,1)} slice(bf16[32,2048]{1,0:T(8,128)(2,1)} %decode_layer.1), slice={[0:20], [0:2048]} | slice | bytes 163840 | tf_op jit(solution)/shard_map/slice | solution.py:631
  (18 shorter events, 0.1 us)

commit v2 on v1

--- a/solution.py
+++ b/solution.py
@@ -178,6 +178,7 @@
     gu_out,
     gu_in,
     active,
+    down_sum,
     load_sem,
     gu_load_sem,
     down_sem,
@@ -278,8 +279,8 @@
 
     first, count = ix("first"), ix("count")
     pool = keys.shape[0]
-    block = tile_of(pool, 512)
-    scale = 1.0 / math.sqrt(head)
+    block = tile_of(pool, 1280)
+    scale = 1.0 / (math.sqrt(head) * math.log(2.0))
     key_load.wait()
     value_load.wait()
 
@@ -297,10 +298,10 @@
                 NT,
                 preferred_element_type=f32,
             )
-            scores = jnp.where(owned, scores * scale, -1e30)
+            scores = jnp.where(owned, scores, -1e30)
             new_top = jnp.maximum(top, jnp.max(scores, axis=1, keepdims=True))
-            shifted = jnp.where(owned, jnp.exp(scores - new_top), 0.0)
-            keep = jnp.exp(top - new_top)
+            shifted = jnp.exp2((scores - new_top) * scale)
+            keep = jnp.exp2((top - new_top) * scale)
             total = total * keep + jnp.sum(shifted, axis=1, keepdims=True)
             out = out * keep + jnp.dot(
                 shifted.astype(bf16), values[pl.ds(at, block), lanes], preferred_element_type=f32
@@ -452,25 +453,26 @@
     active_copies = [
         to_ffn(3, d, active.at[ffn], active.at[ffn]) for d in range(1, n_ffn)
     ]
-    for copy in active_copies:
-        copy.wait()
     widen = one_hot(ix("widen"), requests)
-    for load in down_loads:
-        load.wait()
-
     last_copies = []
-    for c in range(chunks):
-        lanes = slice(c * wide, (c + 1) * wide)
-        product = jnp.dot(active[0], gate_w[:units, lanes], preferred_element_type=f32)
-        for f in range(1, n_ffn):
-            product = product + jnp.dot(
-                active[f], gate_w[f * units : (f + 1) * units, lanes], preferred_element_type=f32
+    for d in range(n_ffn):
+        if d:
+            active_copies[d - 1].wait()
+        down_loads[n_ffn - 1 - d].wait()
+        arrived = active[pl.ds(ffn_peer[d], 1)].reshape(requests, units)
+        for c in range(chunks):
+            lanes = slice(c * wide, (c + 1) * wide)
+            product = jnp.dot(arrived, gate_w[unit_rows[d], lanes], preferred_element_type=f32)
+            if d:
+                product = down_sum[:, lanes] + product
+            if d < n_ffn - 1:
+                down_sum[:, lanes] = product
+                continue
+            product = jnp.dot(widen, product.astype(bf16), preferred_element_type=f32)
+            part_out[:, :, lanes] = product.astype(bf16).reshape(n_att, pad, wide)
+            last_copies.append(
+                [to_owner(c, d, part_out, part_in, last_send, last_recv) for d in range(1, n_att)]
             )
-        product = jnp.dot(widen, product.astype(bf16), preferred_element_type=f32)
-        part_out[:, :, lanes] = product.astype(bf16).reshape(n_att, pad, wide)
-        last_copies.append(
-            [to_owner(c, d, part_out, part_in, last_send, last_recv) for d in range(1, n_att)]
-        )
     for c in range(chunks):
         lanes = slice(c * wide, (c + 1) * wide)
         for copy in last_copies[c]:
@@ -599,6 +601,7 @@
             V((n_ffn - 1, 2, requests, units), bf16),
             V((n_ffn - 1, 2, requests, units), bf16),
             V((n_ffn, requests, units), bf16),
+            V((requests, columns), f32),
             dma((2 + kv_total,)),
             dma((2, n_ffn)),
             dma((n_ffn,)),

time: 118 us -> 112 us (0.949)
  Pallas kernels: 105 us -> 100 us
    pallas_call x1, Pallas kernels: 105 us -> 100 us  [fused_device(): pl.pallas_call(functools.partial(layer_kernel, sizes, places), out_shape=...]
where the time goes in v2:
time: 112 us
  Pallas kernels  100 us (89%)
  local copies, waits for them, and re-layouts  8.64 us (8%)
  other arithmetic  2.83 us (3%)
    pallas_call x1, Pallas kernels, fused_device(): pl.pallas_call(functools.partial(layer_kernel, sizes, places), out_shape=...  100 us

profile of v2, /device:TPU:0, one launch (start us, length us, event | category | flops | bytes accessed | tf_op | source)
XLA Modules:
  0.0 111.9 jit_solution(7941719068028045992)
XLA Ops:
  0.0 0.7 dynamic-slice_multiply_fusion
  0.7 0.8 select_reduce_fusion.1
  1.5 0.8 select_reduce_fusion
  2.3 0.1 broadcast_add_fusion.2
  2.4 0.1 broadcast_add_fusion.1
  2.5 0.1 reshape.221
  2.6 0.1 ge.18
  2.6 0.1 ne.38
  2.7 0.1 add_select_fusion
  2.8 0.1 select_n.61
  2.9 0.1 iota_add_fusion.2
  3.0 0.1 add.208
  3.1 0.1 div.14
  3.2 0.1 rem.24
  3.2 0.1 add_select_fusion.1
  3.3 0.1 broadcast_add_fusion
  3.4 0.1 add.199
  3.5 1.3 %broadcast_in_dim.48.gain_ref = bf16[1,2048]{1,0:T(2,128)(2,1)} reshape(bf16[2048]{0:T(1024)(128)(2,1)} %param.18) | data formatting | bytes 8192 | tf_op jit(solution)/shard_map/broadcast_in_dim | solution.py:625
  4.8 0.1 broadcast_in_dim.78
  4.9 0.1 reshape.219
  5.0 0.7 broadcast_in_dim.79
  5.7 0.1 reshape.220
  5.8 0.1 iota_add_fusion
  5.9 0.1 add.189
  6.0 1.6 %reshape.218.query_ref = bf16[320,128]{1,0:T(8,128)(2,1)} reshape(bf16[20,2048]{1,0:T(8,128)(2,1)} %param.12) | data formatting | bytes 163840 | tf_op jit(solution)/shard_map/reshape | solution.py:564
  7.6 1.6 %pad.30.hidden_ref = bf16[32,2048]{1,0:T(8,128)(2,1)} pad(bf16[20,2048]{1,0:T(8,128)(2,1)} %param.11, bf16[]{:T(256)} %constant.13.clone.1), padding=0_12x0_0 | pad | bytes 212994 | tf_op jit(solution)/shard_map/jit(_pad)/pad | solution.py:565
  9.2 0.8 copy.20.index_ref
  10.0 100.4 %decode_layer.1 = bf16[32,2048]{1,0:T(8,128)(2,1)} custom-call(bf16[320,128]{1,0:T(8,128)(2,1)} %reshape.218.query_ref, bf16[32,2048]{1,0:T(8,128)(2,1)} %pad.30.hidden_ref, bf16[1,2048]{1,0:T(2,128)(2,1)} %broadcast_in_dim.48.gain_ref, s32[512,7]{1,0:T(8,128)} %copy.20.index_ref, bf16[12800,256]{1,0:T(8,128)(2,1)} %key_hbm.1, bf16[12800,256]{1,0:T(8,128)(2,1)} %value_hbm.1, ...), custom_call_target="tpu_custom_call" | custom-call | flops 4194304000 | bytes 65536000 | tf_op jit(solution)/shard_map/decode_layer/pallas_call | solution.py:576
  110.4 1.5 %slice.3 = bf16[20,2048]{1,0:T(8,128)(2,1)} slice(bf16[32,2048]{1,0:T(8,128)(2,1)} %decode_layer.1), slice={[0:20], [0:2048]} | slice | bytes 163840 | tf_op jit(solution)/shard_map/slice | solution.py:634
  (18 shorter events, 0.1 us)
